TPU v7x, 32 devices: a whole 2x2x4 slice. The times are simulated.
32 devices in a mesh: band: 2 (over y), sta: 4 (over z), grid: 4 (over x, core).
Axes of the slice: x: 2, y: 2, z: 4, core: 2. Of those that a mesh axis runs over, the one named last changes fastest.
Arguments:
- green_spectra: float32 [16, 256, 2, 1024], P('band', 'sta', None, 'grid'), parts along dimension 0, may hold values from -6 to 6
- source_power: float32 [16, 1024], P('band', 'grid'), parts along dimension 0, may hold values from 0.25 to 4
- partners: int32 [4, 2], P('sta'), may hold values from 0 to 3, as said below
- observed: float32 [4, 2, 16, 64, 128], P('sta', None, 'band'), parts along dimension 2, may hold values from -6 to 6
- region: int32 [16], P(('band', 'grid')), parts along dimension 0, may hold values 0 or 1
Outputs:
- gradient: float32 [16, 1024], P('band', 'grid'), parts along dimension 0
There are 2 independent parts, one for each index of `band`. A program takes and returns all parts, laid end to end along the dimension named above; an argument that names none is the same for every part. Nothing has to cross between parts.
Inputs may be any that keep to these rules, and one draw needn't show every extreme that they name: `partners`: row a lists 2 distinct blocks, each within loop distance 1 of a among the 4 blocks (block b is at distance min((b - a) mod 4, (a - b) mod 4)); a itself is always listed, and so is one block at distance exactly 1.
All inputs are finite; a program needn't handle non-finite values. No bound on the sum of `region` on one device may be relied on, other than what follows from the above.
Results may differ from a plain program's by a relative error of at most 0.0003.
Values sent between devices are 32-bit elements; how exact they have to be, the bound alone decides.
A program may use at most 64 MiB of HBM per device.

v0:
```python
import math

import jax
import jax.numpy as jnp
from jax import lax
from jax.sharding import PartitionSpec as P

MBLK = 128


HIGH = lax.Precision.HIGHEST


def shifted(block, axis, distance):
    devices = range(lax.axis_size(axis))
    route = [((i - distance) % len(devices), i) for i in devices]
    return lax.ppermute(block, axis, route)


def correlate(scaled, far, norm_scale):
    left_re = scaled[:, :, 0]
    left_im = scaled[:, :, 1]
    right_re = far[:, :, 0]
    right_im = far[:, :, 1]
    real_part = jnp.einsum("fit,fjt->fij", left_re, right_re, precision=HIGH) + jnp.einsum(
        "fit,fjt->fij", left_im, right_im, precision=HIGH
    )
    imag_part = jnp.einsum("fit,fjt->fij", left_im, right_re, precision=HIGH) - jnp.einsum(
        "fit,fjt->fij", left_re, right_im, precision=HIGH
    )
    return jnp.concatenate([real_part, imag_part], axis=-1) * norm_scale


def gradient_term(residual, near, far):
    width = residual.shape[1]
    res_re = residual[..., :width]
    res_im = residual[..., width:]
    near_re = near[:, :, 0]
    near_im = near[:, :, 1]
    mix_re = jnp.einsum("fij,fit->fjt", res_re, near_re, precision=HIGH) + jnp.einsum(
        "fij,fit->fjt", res_im, near_im, precision=HIGH
    )
    mix_im = jnp.einsum("fij,fit->fjt", res_re, near_im, precision=HIGH) - jnp.einsum(
        "fij,fit->fjt", res_im, near_re, precision=HIGH
    )
    return jnp.sum(mix_re * far[:, :, 0] + mix_im * far[:, :, 1], axis=1)


def shards(green_spectra, source_power, partners, observed, region):
    blocks = lax.axis_size("sta")
    own_index = lax.axis_index("sta")
    reach_blocks = min(4, (blocks - 1) // 2)
    pair_count = partners.shape[1]
    block_size = green_spectra.shape[1]
    tile_size = green_spectra.shape[3]
    norm_scale = 1.0 / math.sqrt(tile_size * lax.axis_size("grid"))
    scaled = green_spectra * source_power[:, None, None, :]
    received = {0: green_spectra}
    moving = shifted(green_spectra, "sta", reach_blocks)
    received[-reach_blocks] = moving
    for offset in range(1 - reach_blocks, reach_blocks + 1):
        moving = shifted(moving, "sta", -1)
        if offset != 0:
            received[offset] = moving
    offsets = list(range(-reach_blocks, reach_blocks + 1))
    correlations = jnp.stack(
        [correlate(scaled, received[offset], norm_scale) for offset in offsets]
    )
    targets = (own_index + jnp.arange(-reach_blocks, reach_blocks + 1, dtype=jnp.int32)) % blocks
    select = (partners[0][:, None] == targets[None, :]).astype(jnp.float32)
    pair_terms = jnp.einsum("qk,kfij->qfij", select, correlations, precision=HIGH)
    eyes = jnp.concatenate(
        [jnp.eye(block_size, dtype=jnp.float32), jnp.eye(block_size, dtype=jnp.float32)], axis=1
    )
    self_pair = (partners[0] == own_index).astype(jnp.float32)
    totals = lax.psum(pair_terms, "grid")
    keep = 1.0 - self_pair[:, None, None, None] * eyes[None, None]
    residual = (totals - observed[0]) * keep
    per_offset = jnp.einsum("qk,qfij->kfij", select, residual, precision=HIGH)
    total = jnp.zeros((green_spectra.shape[0], tile_size), jnp.float32)
    for number, offset in enumerate(offsets):
        total = total + gradient_term(per_offset[number], green_spectra, received[offset])
    summed = lax.psum(total, "sta")
    mask = jnp.repeat(region.astype(jnp.float32), MBLK)
    return summed * (norm_scale / math.sqrt(pair_count * block_size)) * mask[None, :]


def solution(mesh):
    in_specs = (
        P("band", "sta", None, "grid"),
        P("band", "grid"),
        P("sta", None),
        P("sta", None, "band", None, None),
        P(("band", "grid")),
    )
    out_specs = P("band", "grid")
    return jax.shard_map(shards, mesh=mesh, in_specs=in_specs, out_specs=out_specs, check_vma=False)
```

profile of v0, /device:TPU:0, one launch (start us, length us, event | category | flops | bytes accessed | tf_op | source)
XLA Modules:
  0.0 156.7 jit_solution(3535437592054691447)
XLA Ops:
  6.5 1.5 broadcast_multiply_fusion
  8.0 3.1 %collective-permute-start = (f32[8,64,2,256]{3,1,0,2:T(8,128)S(1)}, f32[8,64,2,256]{3,1,0,2:T(8,128)S(1)}, u32[]{:S(2)}, u32[]{:S(2)}) collective-permute-start(f32[8,64,2,256]{3,1,0,2:T(8,128)S(1)} %get-tuple-element.9), channel_id=1, source_target_pairs={{12,0},{0,4},{4,8},{8,12},{13,1},{1,5},{5,9},{9,13},{14,2},{2,6},{... | collective-permute-start | bytes 3145736 | tf_op jit(solution)/shard_map/ppermute | solution.py:17
  13.0 23.3 %collective-permute-done = f32[8,64,2,256]{3,1,0,2:T(8,128)S(1)} collective-permute-done((f32[8,64,2,256]{3,1,0,2:T(8,128)S(1)}, f32[8,64,2,256]{3,1,0,2:T(8,128)S(1)}, u32[]{:S(2)}, u32[]{:S(2)}) %collective-permute-start) | collective-permute-done | bytes 1048608 | tf_op jit(solution)/shard_map/ppermute | solution.py:17
  36.3 1.7 %collective-permute-start.1 = (f32[8,64,2,256]{3,1,0,2:T(8,128)S(1)}, f32[8,64,2,256]{3,1,0,2:T(8,128)S(1)}, u32[]{:S(2)}, u32[]{:S(2)}) collective-permute-start(f32[8,64,2,256]{3,1,0,2:T(8,128)S(1)} %collective-permute-done), channel_id=1, source_target_pairs={{4,0},{8,4},{12,8},{0,12},{5,1},{9,5},{13,9},{1,13},{6,2},{10,6},{... | collective-permute-start | bytes 3145736 | tf_op jit(solution)/shard_map/ppermute | solution.py:17
  40.1 20.6 %collective-permute-done.1 = f32[8,64,2,256]{3,1,0,2:T(8,128)S(1)} collective-permute-done((f32[8,64,2,256]{3,1,0,2:T(8,128)S(1)}, f32[8,64,2,256]{3,1,0,2:T(8,128)S(1)}, u32[]{:S(2)}, u32[]{:S(2)}) %collective-permute-start.1) | collective-permute-done | bytes 1048608 | tf_op jit(solution)/shard_map/ppermute | solution.py:17
  60.6 3.2 %collective-permute-start.2 = (f32[8,64,2,256]{3,1,0,2:T(8,128)S(1)}, f32[8,64,2,256]{3,1,0,2:T(8,128)S(1)}, u32[]{:S(2)}, u32[]{:S(2)}) collective-permute-start(f32[8,64,2,256]{3,1,0,2:T(8,128)S(1)} %collective-permute-done.1), channel_id=1, source_target_pairs={{4,0},{8,4},{12,8},{0,12},{5,1},{9,5},{13,9},{1,13},{6,2},{10,6},{... | collective-permute-start | bytes 3145736 | tf_op jit(solution)/shard_map/ppermute | solution.py:17
  66.5 18.0 %collective-permute-done.2 = f32[8,64,2,256]{3,1,0,2:T(8,128)S(1)} collective-permute-done((f32[8,64,2,256]{3,1,0,2:T(8,128)S(1)}, f32[8,64,2,256]{3,1,0,2:T(8,128)S(1)}, u32[]{:S(2)}, u32[]{:S(2)}) %collective-permute-start.2) | collective-permute-done | bytes 1048608 | tf_op jit(solution)/shard_map/ppermute | solution.py:17
  87.2 1.4 fusion.18
  88.7 0.9 copy.25
  89.7 35.1 %all-reduce.2.cloned.1.call-done = f32[2,8,64,128]{3,2,1,0:T(8,128)} async-done(((f32[2,8,64,128]{3,2,1,0:T(8,128)}), f32[2,8,64,128]{3,2,1,0:T(8,128)}) %all-reduce.2.cloned.1.call-update) | async-done | bytes 524304 | tf_op jit(solution)/shard_map/psum | solution.py:76
  124.8 1.1 fusion.20
  125.9 1.5 fusion.21
  127.5 0.7 fusion.56
  128.2 0.7 fusion.32
  128.9 0.7 fusion.29
  130.2 0.7 fusion.31
  130.9 0.9 fusion.30
  132.5 0.7 fusion.5
  133.2 0.8 fusion.10
  134.4 0.7 fusion
  135.1 0.7 fusion.6
  135.9 0.8 fusion.11
  136.6 0.8 fusion.9
  137.4 11.8 %psum.15 = f32[8,256]{1,0:T(8,128)S(1)} all-reduce(f32[8,256]{1,0:T(8,128)S(1)} %add_add_fusion), channel_id=1, replica_groups=mesh['band'=2,'sta'=4,'grid'=4] {'sta'}, use_global_device_ids=true, to_apply=%region_4.5 | all-reduce | flops 2048 | bytes 16384 | tf_op jit(solution)/shard_map/psum | solution.py:83
  (39 shorter events, 11.7 us)
Async XLA Ops:
  6.5 118.3 %all-reduce.2.cloned.1.call-start = ((), (), s32[]{:S(2)}) async-start(), calls=%async_computation | async-start | bytes 1048576 | tf_op jit(solution)/shard_map/psum | solution.py:76
  8.0 28.3 %collective-permute-start = (f32[8,64,2,256]{3,1,0,2:T(8,128)S(1)}, f32[8,64,2,256]{3,1,0,2:T(8,128)S(1)}, u32[]{:S(2)}, u32[]{:S(2)}) collective-permute-start(f32[8,64,2,256]{3,1,0,2:T(8,128)S(1)} %get-tuple-element.9), channel_id=1, source_target_pairs={{12,0},{0,4},{4,8},{8,12},{13,1},{1,5},{5,9},{9,13},{14,2},{2,6},{... | collective-permute-start | bytes 3145736 | tf_op jit(solution)/shard_map/ppermute | solution.py:17
  36.3 24.3 %collective-permute-start.1 = (f32[8,64,2,256]{3,1,0,2:T(8,128)S(1)}, f32[8,64,2,256]{3,1,0,2:T(8,128)S(1)}, u32[]{:S(2)}, u32[]{:S(2)}) collective-permute-start(f32[8,64,2,256]{3,1,0,2:T(8,128)S(1)} %collective-permute-done), channel_id=1, source_target_pairs={{4,0},{8,4},{12,8},{0,12},{5,1},{9,5},{13,9},{1,13},{6,2},{10,6},{... | collective-permute-start | bytes 3145736 | tf_op jit(solution)/shard_map/ppermute | solution.py:17
  38.7 0.7 copy-start.4
  39.3 0.7 copy-start.3
  60.6 23.8 %collective-permute-start.2 = (f32[8,64,2,256]{3,1,0,2:T(8,128)S(1)}, f32[8,64,2,256]{3,1,0,2:T(8,128)S(1)}, u32[]{:S(2)}, u32[]{:S(2)}) collective-permute-start(f32[8,64,2,256]{3,1,0,2:T(8,128)S(1)} %collective-permute-done.1), channel_id=1, source_target_pairs={{4,0},{8,4},{12,8},{0,12},{5,1},{9,5},{13,9},{1,13},{6,2},{10,6},{... | collective-permute-start | bytes 3145736 | tf_op jit(solution)/shard_map/ppermute | solution.py:17
  84.5 1.9 %copy-start = (f32[8,64,2,256]{3,1,0,2:T(8,128)}, f32[8,64,2,256]{3,1,0,2:T(8,128)S(1)}, u32[]{:S(2)}) copy-start(f32[8,64,2,256]{3,1,0,2:T(8,128)S(1)} %collective-permute-done.2) | copy-start | bytes 3145732
  89.5 35.3 %copy-start.2 = (f32[1,2,8,64,128]{4,3,2,1,0:T(8,128)S(1)}, f32[1,2,8,64,128]{4,3,2,1,0:T(8,128)}, u32[]{:S(2)}) copy-start(f32[1,2,8,64,128]{4,3,2,1,0:T(8,128)} %param.8) | copy-start | bytes 1572868
  133.2 1.2 copy-start.1
Sparse Core Ops, SparseCore 0:
  89.7 35.1 all-reduce.1
where the time goes:
time: 157 us
  waiting for transfers between devices  97 us (62%)
  matrix products  19 us (12%)
  between operations  13.7 us (9%)
  blocking collectives  11.8 us (8%)
  starting transfers between devices  8.04 us (5%)
  other arithmetic  3.85 us (2%)
  local copies, waits for them, and re-layouts  3.3 us (2%)
    ppermute x3, waiting for transfers between devices, shifted(): return lax.ppermute(block, axis, route)  61.8 us
    psum x1, waiting for transfers between devices, shards(): totals = lax.psum(pair_terms, 'grid')  35.1 us
    psum x1, blocking collectives, shards(): summed = lax.psum(total, 'sta')  11.8 us
    ppermute x3, starting transfers between devices, shifted(): return lax.ppermute(block, axis, route)  8.04 us
  transfers between devices with their start and end apart: 4, of which 4 were waited for; matrix products, arithmetic and copies ran while one was open for 4% of the time, Pallas kernels for 0%

commit v1 on v0

v1 whole, which is shorter than its diff:
```python
import functools
import math

import jax
import jax.numpy as jnp
from jax import lax
from jax.experimental import pallas as pl
from jax.experimental.pallas import tpu as pltpu
from jax.sharding import PartitionSpec as P

MBLK = 128
MAX_REACH = 4
MESH = pl.DeviceIdType.MESH
F32 = jnp.float32
BF16 = jnp.bfloat16


def split(x):
    high = x.astype(BF16)
    return high, (x - high.astype(F32)).astype(BF16)


def dot3(left, right, contract):
    dot = functools.partial(
        lax.dot_general, dimension_numbers=(contract, ((), ())), preferred_element_type=F32
    )
    return dot(left[0], right[0]) + dot(left[0], right[1]) + dot(left[1], right[0])


def kernel(
    stations, tiles, reach, c_scale, out_scale,
    g_hbm, power_ref, partners_ref, obs_ref, region_ref, out_ref,
    near, far, wide, cpart, crecv, rfull, flip, pay, payrecv, tot, totrecv,
    load_sem, g_send, g_recv, pay_send, pay_recv, c_send, c_recv, r_send, r_recv, t_send, t_recv,
):
    freqs, rows, _ = g_hbm.shape
    block = obs_ref.shape[3]
    pairs = obs_ref.shape[1]
    cols = rows // (2 * block)
    tile = cols * 128
    own_rows = block // tiles
    me = lax.axis_index("sta")
    mine = lax.axis_index("grid")
    first = pl.multiple_of(mine * own_rows, own_rows)

    load = pltpu.make_async_copy(g_hbm, near, load_sem)
    load.start()

    barrier = pltpu.get_barrier_semaphore()
    for k in range(1, stations):
        pl.semaphore_signal(
            barrier, inc=1, device_id={"sta": lax.rem(me + k, stations)}, device_id_type=MESH
        )
    for k in range(1, tiles):
        pl.semaphore_signal(
            barrier, inc=1, device_id={"grid": lax.rem(mine + k, tiles)}, device_id_type=MESH
        )
    pl.semaphore_wait(barrier, stations - 1 + tiles - 1)

    def green_copy(d, f):
        return pltpu.make_async_remote_copy(
            src_ref=g_hbm.at[f], dst_ref=far.at[d - 1, f],
            send_sem=g_send.at[d - 1, f], recv_sem=g_recv.at[d - 1, f],
            device_id={"sta": lax.rem(me + d, stations)}, device_id_type=MESH,
        )

    def pay_copy(d):
        return pltpu.make_async_remote_copy(
            src_ref=pay.at[d - 1], dst_ref=payrecv.at[d - 1],
            send_sem=pay_send.at[d - 1], recv_sem=pay_recv.at[d - 1],
            device_id={"sta": lax.rem(me + d, stations)}, device_id_type=MESH,
        )

    def corr_copy(k, f):
        peer = lax.rem(mine + k, tiles)
        return pltpu.make_async_remote_copy(
            src_ref=cpart.at[f, peer], dst_ref=crecv.at[f, k],
            send_sem=c_send.at[k, f], recv_sem=c_recv.at[k, f],
            device_id={"grid": peer}, device_id_type=MESH,
        )

    def resid_copy(k, f, owner):
        return pltpu.make_async_remote_copy(
            src_ref=rfull.at[f, owner], dst_ref=rfull.at[f, owner],
            send_sem=r_send.at[k, f], recv_sem=r_recv.at[k, f],
            device_id={"grid": lax.rem(mine + k, tiles)}, device_id_type=MESH,
        )

    def total_copy(k):
        return pltpu.make_async_remote_copy(
            src_ref=tot, dst_ref=totrecv.at[k],
            send_sem=t_send.at[k], recv_sem=t_recv.at[k],
            device_id={"sta": lax.rem(me + k, stations)}, device_id_type=MESH,
        )

    def listed(q, target):
        return jnp.where(partners_ref[0, q] == target, 1.0, 0.0).astype(F32)

    early = min(2, freqs)
    for f in range(early):
        for d in range(1, reach + 1):
            green_copy(d, f).start()

    lane = lax.broadcasted_iota(jnp.int32, (own_rows, 2 * block), 1)
    sign = jnp.where(lane < block, 1.0, -1.0).astype(F32)
    for d in range(1, reach + 1):
        target = lax.rem(me + d, stations)
        flags = [listed(q, target) for q in range(pairs)]

        def flip_one(f, carry):
            chosen = flags[0] * obs_ref[0, 0, f]
            for q in range(1, pairs):
                chosen = chosen + flags[q] * obs_ref[0, q, f]
            square = jnp.concatenate([chosen, pltpu.roll(chosen, block, 1)], axis=0)
            flip[...] = square.T
            pay[d - 1, f] = flip[pl.ds(first, own_rows), :] * sign
            return carry

        lax.fori_loop(0, freqs, flip_one, 0)
        count = flags[0]
        for q in range(1, pairs):
            count = count + flags[q]
        pay[d - 1, freqs] = jnp.zeros((own_rows, 2 * block), F32) + count
        pay_copy(d).start()

    for f in range(early, freqs):
        for d in range(1, reach + 1):
            green_copy(d, f).start()

    load.wait()

    def parts(ref, f):
        out = []
        for part in range(2):
            pieces = [
                ref[f, pl.ds(2 * c + part, block, stride=2 * cols), :] for c in range(cols)
            ]
            out.append(jnp.concatenate(pieces, axis=1))
        return out

    def widen(real, imag, slot, f):
        rh, rl = split(real)
        ih, il = split(imag)
        for number, (re, im) in enumerate(((rh, ih), (rl, il))):
            wide[slot, f, number, 0:block] = jnp.concatenate([re, im], axis=1)
            wide[slot, f, number, block : 2 * block] = jnp.concatenate([-im, re], axis=1)

    def correlate(left, slot, f):
        right = (wide[slot, f, 0], wide[slot, f, 1])
        whole = dot3(left, right, ((1,), (1,))) * c_scale
        for k in range(tiles):
            cpart[f, k, slot] = whole[k * own_rows : (k + 1) * own_rows]

    def stage_corr(f):
        real, imag = parts(near, f)
        power = power_ref[pl.ds(f, 1), :]
        widen(real, imag, 0, f)
        left = split(jnp.concatenate([real * power, imag * power], axis=1))
        correlate(left, 0, f)
        for d in range(1, reach + 1):
            green_copy(d, f).wait_recv()
            real, imag = parts(far.at[d - 1], f)
            widen(real, imag, d, f)
            correlate(left, d, f)
        for k in range(1, tiles):
            corr_copy(k, f).start()

    row = lax.broadcasted_iota(jnp.int32, (own_rows, 2 * block), 0) + mine * own_rows
    keep = jnp.where(lax.rem(lane, block) == row, 0.0, 1.0).astype(F32)

    def observed_rows(f, target):
        chosen = listed(0, target) * obs_ref[0, 0, f, pl.ds(first, own_rows), :]
        for q in range(1, pairs):
            chosen = chosen + listed(q, target) * obs_ref[0, q, f, pl.ds(first, own_rows), :]
        return chosen

    def stage_resid(f):
        for k in range(1, tiles):
            corr_copy(k, f).wait_recv()
        for slot in range(reach + 1):
            total = cpart[f, mine, slot]
            for k in range(1, tiles):
                total = total + crecv[f, k, slot]
            target = lax.rem(me + stations - slot, stations)
            seen = observed_rows(f, target)
            if slot == 0:
                result = (total - seen) * keep
            else:
                weight = payrecv[slot - 1, freqs]
                for q in range(pairs):
                    weight = weight + listed(q, target)
                result = weight * total - (seen + payrecv[slot - 1, f])
            rfull[f, mine, slot] = result
        for k in range(1, tiles):
            resid_copy(k, f, mine).start()

    def stage_grad(f):
        for k in range(1, tiles):
            resid_copy(k, f, lax.rem(mine + tiles - k, tiles)).wait_recv()
        mixed = None
        for slot in range(reach + 1):
            resid = jnp.concatenate([rfull[f, k, slot] for k in range(tiles)], axis=0)
            term = dot3(split(resid), (wide[slot, f, 0], wide[slot, f, 1]), ((1,), (0,)))
            mixed = term if mixed is None else mixed + term
        real, imag = parts(near, f)
        line = jnp.sum(real * mixed[:, :tile] + imag * mixed[:, tile:], axis=0, keepdims=True)
        tot[pl.ds(f, 1), :] = line

    def step(s, carry):
        @pl.when(s < freqs)
        def _():
            stage_corr(s)

        @pl.when(s == 1)
        def _():
            for d in range(1, reach + 1):
                pay_copy(d).wait_recv()

        @pl.when(jnp.logical_and(s >= 1, s < freqs + 1))
        def _():
            stage_resid(s - 1)

        @pl.when(s >= 2)
        def _():
            stage_grad(s - 2)

        return carry

    lax.fori_loop(0, freqs + 2, step, 0)

    for k in range(1, stations):
        total_copy(k).start()

    def drain(f, carry):
        for d in range(1, reach + 1):
            green_copy(d, f).wait_send()
        for k in range(1, tiles):
            corr_copy(k, f).wait_send()
            resid_copy(k, f, mine).wait_send()
        return carry

    lax.fori_loop(0, freqs, drain, 0)
    for d in range(1, reach + 1):
        pay_copy(d).wait_send()
    summed = tot[...]
    for k in range(1, stations):
        total_copy(k).wait_recv()
        summed = summed + totrecv[k]
    for c in range(tile // MBLK):
        factor = region_ref[c].astype(F32) * out_scale
        span = slice(c * MBLK, (c + 1) * MBLK)
        out_ref[:, span] = summed[:, span] * factor
    for k in range(1, stations):
        total_copy(k).wait_send()


def shards(green_spectra, source_power, partners, observed, region):
    stations = lax.axis_size("sta")
    tiles = lax.axis_size("grid")
    reach = min(MAX_REACH, (stations - 1) // 2)
    freqs, block, _, tile = green_spectra.shape
    pairs = partners.shape[1]
    cols = tile // 128
    own_rows = block // tiles
    slots = reach + 1
    c_scale = 1.0 / math.sqrt(tile * tiles)
    out_scale = c_scale / math.sqrt(pairs * block)
    green = green_spectra.reshape(freqs, block, 2, cols, 128)
    green = green.transpose(0, 1, 3, 2, 4).reshape(freqs, block * cols * 2, 128)
    vmem = pl.BlockSpec(memory_space=pltpu.VMEM)
    smem = pl.BlockSpec(memory_space=pltpu.SMEM)
    dma = pltpu.SemaphoreType.DMA
    return pl.pallas_call(
        functools.partial(kernel, stations, tiles, reach, c_scale, out_scale),
        out_shape=jax.ShapeDtypeStruct((freqs, tile), F32),
        in_specs=[pl.BlockSpec(memory_space=pl.ANY), vmem, smem, vmem, smem],
        out_specs=vmem,
        scratch_shapes=[
            pltpu.VMEM(green.shape, F32),
            pltpu.VMEM((reach,) + green.shape, F32),
            pltpu.VMEM((slots, freqs, 2, 2 * block, 2 * tile), BF16),
            pltpu.VMEM((freqs, tiles, slots, own_rows, 2 * block), F32),
            pltpu.VMEM((freqs, tiles, slots, own_rows, 2 * block), F32),
            pltpu.VMEM((freqs, tiles, slots, own_rows, 2 * block), F32),
            pltpu.VMEM((2 * block, 2 * block), F32),
            pltpu.VMEM((reach, freqs + 1, own_rows, 2 * block), F32),
            pltpu.VMEM((reach, freqs + 1, own_rows, 2 * block), F32),
            pltpu.VMEM((freqs, tile), F32),
            pltpu.VMEM((stations, freqs, tile), F32),
            dma,
            dma((reach, freqs)), dma((reach, freqs)),
            dma((reach,)), dma((reach,)),
            dma((tiles, freqs)), dma((tiles, freqs)),
            dma((tiles, freqs)), dma((tiles, freqs)),
            dma((stations,)), dma((stations,)),
        ],
        compiler_params=pltpu.CompilerParams(
            collective_id=0, has_side_effects=True, vmem_limit_bytes=48 * 1024 * 1024
        ),
    )(green, source_power, partners, observed, region)


def solution(mesh):
    in_specs = (
        P("band", "sta", None, "grid"),
        P("band", "grid"),
        P("sta", None),
        P("sta", None, "band", None, None),
        P(("band", "grid")),
    )
    out_specs = P("band", "grid")
    return jax.shard_map(shards, mesh=mesh, in_specs=in_specs, out_specs=out_specs, check_vma=False)
```

time: 157 us -> 46.3 us (0.29)
  waiting for transfers between devices: 97 us -> 0 us
  Pallas kernels: 0 us -> 41.8 us
  matrix products: 19 us -> 0 us
  between operations: 13.7 us -> 0.01 us
  blocking collectives: 11.8 us -> 0 us
  starting transfers between devices: 8.04 us -> 0 us
  other arithmetic: 3.85 us -> 0 us
    ppermute x3 -> x0, waiting for transfers between devices: 61.8 us -> none  [shifted(): return lax.ppermute(block, axis, route)]
    pallas_call x0 -> x1, Pallas kernels: none -> 41.8 us  [shards(): pl.pallas_call(functools.partial(kernel, stations, tiles, reach, c_scale,...]
    psum x1 -> x0, waiting for transfers between devices: 35.1 us -> none  [shards(): totals = lax.psum(pair_terms, 'grid')]
    dot_general x26 -> x0, matrix products: 19 us -> none  [the longest x3 2.23 us: gradient_term(): jnp.einsum('fij,fit->fjt', res_re, near_re, precision=HIGH)]
    psum x1 -> x0, blocking collectives: 11.8 us -> none  [shards(): summed = lax.psum(total, 'sta')]
    ppermute x3 -> x0, starting transfers between devices: 8.04 us -> none  [shifted(): return lax.ppermute(block, axis, route)]
    mul x7 -> x0, other arithmetic: 3.6 us -> none  [the longest x1 1.48 us: shards(): scaled = green_spectra * source_power[:, None, None, :]]
    unnamed x10 -> x11, local copies, waits for them, and re-layouts: 1.63 us -> 4.23 us
  transfers between devices with their start and end apart: 4 -> 0, of which waited for: 4 -> 0; matrix products, arithmetic and copies ran while one was open for 4% -> 0% of each run, Pallas kernels for 0% -> 0%
where the time goes in v1:
time: 46.3 us; the launch traced here: 46.1 us
  Pallas kernels  41.8 us (90%)
  local copies, waits for them, and re-layouts  4.23 us (9%)
    pallas_call x1, Pallas kernels, shards(): pl.pallas_call(functools.partial(kernel, stations, tiles, reach, c_scale,...  41.8 us
    unnamed x11, local copies, waits for them, and re-layouts  4.23 us

profile of v1, /device:TPU:0, one launch (start us, length us, event | category | flops | bytes accessed | tf_op | source)
XLA Modules:
  0.0 46.1 jit_solution(18137557753807739476)
XLA Ops:
  0.0 0.0 copy-start.4
  0.0 0.0 copy-start.3
  0.0 0.7 %copy-done.4 = s32[2]{0:T(128)S(1)} copy-done((s32[2]{0:T(128)S(1)}, s32[2]{0:T(128)}, u32[]{:S(2)}) %copy-start.4) | copy-done | bytes 32
  0.7 0.0 copy-done.3
  0.7 0.0 copy-start
  0.7 1.2 %copy-done = f32[8,64,2,256]{3,2,1,0:T(2,128)S(1)} copy-done((f32[8,64,2,256]{3,2,1,0:T(2,128)S(1)}, f32[8,64,2,256]{3,2,1,0:T(2,128)}, u32[]{:S(2)}) %copy-start) | copy-done | bytes 1048600
  1.9 0.0 copy-start.1
  1.9 1.0 %copy-done.1 = f32[1,2,8,64,128]{4,3,2,1,0:T(8,128)S(1)} copy-done((f32[1,2,8,64,128]{4,3,2,1,0:T(8,128)S(1)}, f32[1,2,8,64,128]{4,3,2,1,0:T(8,128)}, u32[]{:S(2)}) %copy-start.1) | copy-done | bytes 524312
  2.9 0.0 copy-start.2
  2.9 0.7 %copy-done.2 = f32[8,256]{1,0:T(8,128)S(1)} copy-done((f32[8,256]{1,0:T(8,128)S(1)}, f32[8,256]{1,0:T(8,128)}, u32[]{:S(2)}) %copy-start.2) | copy-done | bytes 8216
  3.6 41.8 %shard_map.55 = f32[8,256]{1,0:T(8,128)S(1)} custom-call(f32[8,256,128]{2,1,0:T(8,128)S(1)} %bitcast.5, f32[8,256]{1,0:T(8,128)S(1)} %copy-done.2, s32[1,2]{1,0:T(1,128)S(1)} %copy-done.3, f32[1,2,8,64,128]{4,3,2,1,0:T(8,128)S(1)} %copy-done.1, s32[2]{0:T(128)S(1)} %copy-done.4), custom_call_target="tpu_custom_call" | custom-call | tf_op jit(solution)/shard_map/pallas_call | solution.py:273
  45.5 0.6 %copy.8 = f32[8,256]{1,0:T(8,128)} copy(f32[8,256]{1,0:T(8,128)S(1)} %shard_map.55) | data formatting | bytes 16384
Async XLA Ops:
  0.0 0.7 %copy-start.4 = (s32[2]{0:T(128)S(1)}, s32[2]{0:T(128)}, u32[]{:S(2)}) copy-start(s32[2]{0:T(128)} %region_ref.1) | copy-start | bytes 28
  0.0 0.7 %copy-start.3 = (s32[1,2]{1,0:T(1,128)S(1)}, s32[1,2]{1,0:T(1,128)}, u32[]{:S(2)}) copy-start(s32[1,2]{1,0:T(1,128)} %partners_ref.1) | copy-start | bytes 28
  0.7 1.2 %copy-start = (f32[8,64,2,256]{3,2,1,0:T(2,128)S(1)}, f32[8,64,2,256]{3,2,1,0:T(2,128)}, u32[]{:S(2)}) copy-start(f32[8,64,2,256]{3,2,1,0:T(2,128)} %param.5) | copy-start | bytes 3145732
  1.9 1.0 %copy-start.1 = (f32[1,2,8,64,128]{4,3,2,1,0:T(8,128)S(1)}, f32[1,2,8,64,128]{4,3,2,1,0:T(8,128)}, u32[]{:S(2)}) copy-start(f32[1,2,8,64,128]{4,3,2,1,0:T(8,128)} %obs_ref.1) | copy-start | bytes 1572868
  2.9 0.7 %copy-start.2 = (f32[8,256]{1,0:T(8,128)S(1)}, f32[8,256]{1,0:T(8,128)}, u32[]{:S(2)}) copy-start(f32[8,256]{1,0:T(8,128)} %power_ref.1) | copy-start | bytes 24580

commit v2 on v1

--- a/solution.py
+++ b/solution.py
@@ -29,9 +29,9 @@
 
 def kernel(
     stations, tiles, reach, c_scale, out_scale,
-    g_hbm, power_ref, partners_ref, obs_ref, region_ref, out_ref,
-    near, far, wide, cpart, crecv, rfull, flip, pay, payrecv, tot, totrecv,
-    load_sem, g_send, g_recv, pay_send, pay_recv, c_send, c_recv, r_send, r_recv, t_send, t_recv,
+    g_hbm, power_hbm, partners_hbm, obs_hbm, region_hbm, out_ref,
+    power_ref, partners_ref, obs_ref, region_ref, near, lefts, far, wide, cpart, crecv, rfull, flip, pay, payrecv, tot, totrecv,
+    load_sem, small_sem, g_send, g_recv, pay_send, pay_recv, c_send, c_recv, r_send, r_recv, t_send, t_recv,
 ):
     freqs, rows, _ = g_hbm.shape
     block = obs_ref.shape[3]
@@ -45,6 +45,15 @@
 
     load = pltpu.make_async_copy(g_hbm, near, load_sem)
     load.start()
+    small = [
+        pltpu.make_async_copy(source, target, small_sem.at[number])
+        for number, (source, target) in enumerate((
+            (partners_hbm, partners_ref), (obs_hbm, obs_ref),
+            (power_hbm, power_ref), (region_hbm, region_ref),
+        ))
+    ]
+    for copy in small:
+        copy.start()
 
     barrier = pltpu.get_barrier_semaphore()
     for k in range(1, stations):
@@ -100,6 +109,9 @@
     for f in range(early):
         for d in range(1, reach + 1):
             green_copy(d, f).start()
+
+    for copy in small:
+        copy.wait()
 
     lane = lax.broadcasted_iota(jnp.int32, (own_rows, 2 * block), 1)
     sign = jnp.where(lane < block, 1.0, -1.0).astype(F32)
@@ -151,12 +163,17 @@
         for k in range(tiles):
             cpart[f, k, slot] = whole[k * own_rows : (k + 1) * own_rows]
 
-    def stage_corr(f):
+    def stage_self(f):
         real, imag = parts(near, f)
         power = power_ref[pl.ds(f, 1), :]
         widen(real, imag, 0, f)
-        left = split(jnp.concatenate([real * power, imag * power], axis=1))
-        correlate(left, 0, f)
+        high, low = split(jnp.concatenate([real * power, imag * power], axis=1))
+        lefts[f, 0] = high
+        lefts[f, 1] = low
+        correlate((high, low), 0, f)
+
+    def stage_cross(f):
+        left = (lefts[f, 0], lefts[f, 1])
         for d in range(1, reach + 1):
             green_copy(d, f).wait_recv()
             real, imag = parts(far.at[d - 1], f)
@@ -206,27 +223,30 @@
         line = jnp.sum(real * mixed[:, :tile] + imag * mixed[:, tile:], axis=0, keepdims=True)
         tot[pl.ds(f, 1), :] = line
 
+    resid_lag, grad_lag = 1, 2
+
     def step(s, carry):
         @pl.when(s < freqs)
         def _():
-            stage_corr(s)
-
-        @pl.when(s == 1)
+            stage_self(s)
+            stage_cross(s)
+
+        @pl.when(s == resid_lag)
         def _():
             for d in range(1, reach + 1):
                 pay_copy(d).wait_recv()
 
-        @pl.when(jnp.logical_and(s >= 1, s < freqs + 1))
+        @pl.when(jnp.logical_and(s >= resid_lag, s < freqs + resid_lag))
         def _():
-            stage_resid(s - 1)
-
-        @pl.when(s >= 2)
+            stage_resid(s - resid_lag)
+
+        @pl.when(s >= grad_lag)
         def _():
-            stage_grad(s - 2)
+            stage_grad(s - grad_lag)
 
         return carry
 
-    lax.fori_loop(0, freqs + 2, step, 0)
+    lax.fori_loop(0, freqs + grad_lag, step, 0)
 
     for k in range(1, stations):
         total_copy(k).start()
@@ -268,15 +288,19 @@
     green = green_spectra.reshape(freqs, block, 2, cols, 128)
     green = green.transpose(0, 1, 3, 2, 4).reshape(freqs, block * cols * 2, 128)
     vmem = pl.BlockSpec(memory_space=pltpu.VMEM)
-    smem = pl.BlockSpec(memory_space=pltpu.SMEM)
     dma = pltpu.SemaphoreType.DMA
     return pl.pallas_call(
         functools.partial(kernel, stations, tiles, reach, c_scale, out_scale),
         out_shape=jax.ShapeDtypeStruct((freqs, tile), F32),
-        in_specs=[pl.BlockSpec(memory_space=pl.ANY), vmem, smem, vmem, smem],
+        in_specs=[pl.BlockSpec(memory_space=pl.ANY)] * 5,
         out_specs=vmem,
         scratch_shapes=[
+            pltpu.VMEM(source_power.shape, F32),
+            pltpu.SMEM(partners.shape, jnp.int32),
+            pltpu.VMEM(observed.shape, F32),
+            pltpu.SMEM(region.shape, jnp.int32),
             pltpu.VMEM(green.shape, F32),
+            pltpu.VMEM((freqs, 2, block, 2 * tile), BF16),
             pltpu.VMEM((reach,) + green.shape, F32),
             pltpu.VMEM((slots, freqs, 2, 2 * block, 2 * tile), BF16),
             pltpu.VMEM((freqs, tiles, slots, own_rows, 2 * block), F32),
@@ -288,6 +312,7 @@
             pltpu.VMEM((freqs, tile), F32),
             pltpu.VMEM((stations, freqs, tile), F32),
             dma,
+            dma((4,)),
             dma((reach, freqs)), dma((reach, freqs)),
             dma((reach,)), dma((reach,)),
             dma((tiles, freqs)), dma((tiles, freqs)),
@@ -295,7 +320,7 @@
             dma((stations,)), dma((stations,)),
         ],
         compiler_params=pltpu.CompilerParams(
-            collective_id=0, has_side_effects=True, vmem_limit_bytes=48 * 1024 * 1024
+            collective_id=0, has_side_effects=True, vmem_limit_bytes=60 * 1024 * 1024
         ),
     )(green, source_power, partners, observed, region)
 

time: 46.3 us -> 43.5 us (0.940)
  local copies, waits for them, and re-layouts: 4.23 us -> 1.3 us
    unnamed x11 -> x1, local copies, waits for them, and re-layouts: 4.23 us -> 1.3 us
where the time goes in v2:
time: 43.5 us; the launch traced here: 43.3 us
  Pallas kernels  42 us (97%)
  local copies, waits for them, and re-layouts  1.3 us (3%)
    pallas_call x1, Pallas kernels, shards(): pl.pallas_call(functools.partial(kernel, stations, tiles, reach, c_scale,...  42 us
    unnamed x1, local copies, waits for them, and re-layouts  1.3 us

profile of v2, /device:TPU:0, one launch (start us, length us, event | category | flops | bytes accessed | tf_op | source)
XLA Modules:
  0.0 43.3 jit_solution(10760720172268648461)
XLA Ops:
  0.0 42.0 %shard_map.55 = f32[8,256]{1,0:T(8,128)} custom-call(f32[8,256,128]{2,1,0:T(8,128)} %bitcast.5, f32[8,256]{1,0:T(8,128)} %power_hbm.1, s32[1,2]{1,0:T(1,128)} %partners_hbm.1, f32[1,2,8,64,128]{4,3,2,1,0:T(8,128)} %obs_hbm.1, s32[2]{0:T(128)} %region_hbm.1), custom_call_target="tpu_custom_call" | custom-call | tf_op jit(solution)/shard_map/pallas_call | solution.py:292
  42.0 1.3 %copy.8 = f32[8,256]{1,0:T(8,128)} copy(f32[8,256]{1,0:T(8,128)} %shard_map.55) | data formatting | bytes 16384

commit v3 on v2

--- a/solution.py
+++ b/solution.py
@@ -28,10 +28,11 @@
 
 
 def kernel(
-    stations, tiles, reach, c_scale, out_scale,
-    g_hbm, power_hbm, partners_hbm, obs_hbm, region_hbm, out_ref,
-    power_ref, partners_ref, obs_ref, region_ref, near, lefts, far, wide, cpart, crecv, rfull, flip, pay, payrecv, tot, totrecv,
-    load_sem, small_sem, g_send, g_recv, pay_send, pay_recv, c_send, c_recv, r_send, r_recv, t_send, t_recv,
+    stations, tiles, reach, c_scale,
+    g_hbm, power_hbm, partners_hbm, obs_hbm, out_ref,
+    power_ref, partners_ref, obs_ref, near, lefts, far, wide, cself, cselfrecv, rself, cpart, crecv, rfull, flip, pay, payrecv, tot,
+    load_sem, small_sem, own_sem, g_send, g_recv, pay_send, pay_recv, cs_send, cs_recv, rs_send, rs_recv,
+    c_send, c_recv, r_send, r_recv, t_send, t_recv,
 ):
     freqs, rows, _ = g_hbm.shape
     block = obs_ref.shape[3]
@@ -43,27 +44,28 @@
     mine = lax.axis_index("grid")
     first = pl.multiple_of(mine * own_rows, own_rows)
 
+    barrier = pltpu.get_barrier_semaphore()
+    for k in range(1, stations):
+        pl.semaphore_signal(
+            barrier, inc=1, device_id={"sta": lax.rem(me + k, stations)}, device_id_type=MESH
+        )
+    for k in range(1, tiles):
+        pl.semaphore_signal(
+            barrier, inc=1, device_id={"grid": lax.rem(mine + k, tiles)}, device_id_type=MESH
+        )
+
     load = pltpu.make_async_copy(g_hbm, near, load_sem)
     load.start()
     small = [
         pltpu.make_async_copy(source, target, small_sem.at[number])
         for number, (source, target) in enumerate((
             (partners_hbm, partners_ref), (obs_hbm, obs_ref),
-            (power_hbm, power_ref), (region_hbm, region_ref),
+            (power_hbm, power_ref),
         ))
     ]
     for copy in small:
         copy.start()
 
-    barrier = pltpu.get_barrier_semaphore()
-    for k in range(1, stations):
-        pl.semaphore_signal(
-            barrier, inc=1, device_id={"sta": lax.rem(me + k, stations)}, device_id_type=MESH
-        )
-    for k in range(1, tiles):
-        pl.semaphore_signal(
-            barrier, inc=1, device_id={"grid": lax.rem(mine + k, tiles)}, device_id_type=MESH
-        )
     pl.semaphore_wait(barrier, stations - 1 + tiles - 1)
 
     def green_copy(d, f):
@@ -95,9 +97,24 @@
             device_id={"grid": lax.rem(mine + k, tiles)}, device_id_type=MESH,
         )
 
+    def self_corr_copy(k):
+        peer = lax.rem(mine + k, tiles)
+        return pltpu.make_async_remote_copy(
+            src_ref=cself.at[peer], dst_ref=cselfrecv.at[k],
+            send_sem=cs_send.at[k], recv_sem=cs_recv.at[k],
+            device_id={"grid": peer}, device_id_type=MESH,
+        )
+
+    def self_resid_copy(k, owner):
+        return pltpu.make_async_remote_copy(
+            src_ref=rself.at[owner], dst_ref=rself.at[owner],
+            send_sem=rs_send.at[k], recv_sem=rs_recv.at[k],
+            device_id={"grid": lax.rem(mine + k, tiles)}, device_id_type=MESH,
+        )
+
     def total_copy(k):
         return pltpu.make_async_remote_copy(
-            src_ref=tot, dst_ref=totrecv.at[k],
+            src_ref=tot, dst_ref=out_ref.at[k],
             send_sem=t_send.at[k], recv_sem=t_recv.at[k],
             device_id={"sta": lax.rem(me + k, stations)}, device_id_type=MESH,
         )
@@ -161,7 +178,11 @@
         right = (wide[slot, f, 0], wide[slot, f, 1])
         whole = dot3(left, right, ((1,), (1,))) * c_scale
         for k in range(tiles):
-            cpart[f, k, slot] = whole[k * own_rows : (k + 1) * own_rows]
+            piece = whole[k * own_rows : (k + 1) * own_rows]
+            if slot == 0:
+                cself[k, f] = piece
+            else:
+                cpart[f, k, slot - 1] = piece
 
     def stage_self(f):
         real, imag = parts(near, f)
@@ -191,23 +212,34 @@
             chosen = chosen + listed(q, target) * obs_ref[0, q, f, pl.ds(first, own_rows), :]
         return chosen
 
+    def self_resid():
+        for k in range(1, tiles):
+            self_corr_copy(k).wait_recv()
+
+        def one(f, carry):
+            total = cself[mine, f]
+            for k in range(1, tiles):
+                total = total + cselfrecv[k, f]
+            rself[mine, f] = (total - observed_rows(f, me)) * keep
+            return carry
+
+        lax.fori_loop(0, freqs, one, 0)
+        for k in range(1, tiles):
+            self_resid_copy(k, mine).start()
+
     def stage_resid(f):
         for k in range(1, tiles):
             corr_copy(k, f).wait_recv()
-        for slot in range(reach + 1):
-            total = cpart[f, mine, slot]
+        for d in range(1, reach + 1):
+            total = cpart[f, mine, d - 1]
             for k in range(1, tiles):
-                total = total + crecv[f, k, slot]
-            target = lax.rem(me + stations - slot, stations)
-            seen = observed_rows(f, target)
-            if slot == 0:
-                result = (total - seen) * keep
-            else:
-                weight = payrecv[slot - 1, freqs]
-                for q in range(pairs):
-                    weight = weight + listed(q, target)
-                result = weight * total - (seen + payrecv[slot - 1, f])
-            rfull[f, mine, slot] = result
+                total = total + crecv[f, k, d - 1]
+            target = lax.rem(me + stations - d, stations)
+            weight = payrecv[d - 1, freqs]
+            for q in range(pairs):
+                weight = weight + listed(q, target)
+            seen = observed_rows(f, target) + payrecv[d - 1, f]
+            rfull[f, mine, d - 1] = weight * total - seen
         for k in range(1, tiles):
             resid_copy(k, f, mine).start()
 
@@ -216,7 +248,8 @@
             resid_copy(k, f, lax.rem(mine + tiles - k, tiles)).wait_recv()
         mixed = None
         for slot in range(reach + 1):
-            resid = jnp.concatenate([rfull[f, k, slot] for k in range(tiles)], axis=0)
+            pieces = [rself[k, f] if slot == 0 else rfull[f, k, slot - 1] for k in range(tiles)]
+            resid = jnp.concatenate(pieces, axis=0)
             term = dot3(split(resid), (wide[slot, f, 0], wide[slot, f, 1]), ((1,), (0,)))
             mixed = term if mixed is None else mixed + term
         real, imag = parts(near, f)
@@ -225,16 +258,29 @@
 
     resid_lag, grad_lag = 1, 2
 
+    def self_one(f, carry):
+        stage_self(f)
+        return carry
+
+    lax.fori_loop(0, freqs, self_one, 0)
+    for k in range(1, tiles):
+        self_corr_copy(k).start()
+
     def step(s, carry):
         @pl.when(s < freqs)
         def _():
-            stage_self(s)
             stage_cross(s)
 
         @pl.when(s == resid_lag)
         def _():
             for d in range(1, reach + 1):
                 pay_copy(d).wait_recv()
+            self_resid()
+
+        @pl.when(s == grad_lag)
+        def _():
+            for k in range(1, tiles):
+                self_resid_copy(k, lax.rem(mine + tiles - k, tiles)).wait_recv()
 
         @pl.when(jnp.logical_and(s >= resid_lag, s < freqs + resid_lag))
         def _():
@@ -250,6 +296,8 @@
 
     for k in range(1, stations):
         total_copy(k).start()
+    keep_own = pltpu.make_async_copy(tot, out_ref.at[0], own_sem)
+    keep_own.start()
 
     def drain(f, carry):
         for d in range(1, reach + 1):
@@ -262,14 +310,12 @@
     lax.fori_loop(0, freqs, drain, 0)
     for d in range(1, reach + 1):
         pay_copy(d).wait_send()
-    summed = tot[...]
+    for k in range(1, tiles):
+        self_corr_copy(k).wait_send()
+        self_resid_copy(k, mine).wait_send()
+    keep_own.wait()
     for k in range(1, stations):
         total_copy(k).wait_recv()
-        summed = summed + totrecv[k]
-    for c in range(tile // MBLK):
-        factor = region_ref[c].astype(F32) * out_scale
-        span = slice(c * MBLK, (c + 1) * MBLK)
-        out_ref[:, span] = summed[:, span] * factor
     for k in range(1, stations):
         total_copy(k).wait_send()
 
@@ -287,34 +333,37 @@
     out_scale = c_scale / math.sqrt(pairs * block)
     green = green_spectra.reshape(freqs, block, 2, cols, 128)
     green = green.transpose(0, 1, 3, 2, 4).reshape(freqs, block * cols * 2, 128)
-    vmem = pl.BlockSpec(memory_space=pltpu.VMEM)
     dma = pltpu.SemaphoreType.DMA
-    return pl.pallas_call(
-        functools.partial(kernel, stations, tiles, reach, c_scale, out_scale),
-        out_shape=jax.ShapeDtypeStruct((freqs, tile), F32),
-        in_specs=[pl.BlockSpec(memory_space=pl.ANY)] * 5,
-        out_specs=vmem,
+    totals = pl.pallas_call(
+        functools.partial(kernel, stations, tiles, reach, c_scale),
+        out_shape=jax.ShapeDtypeStruct((stations, freqs, tile), F32),
+        in_specs=[pl.BlockSpec(memory_space=pl.ANY)] * 4,
+        out_specs=pl.BlockSpec(memory_space=pl.ANY),
         scratch_shapes=[
             pltpu.VMEM(source_power.shape, F32),
             pltpu.SMEM(partners.shape, jnp.int32),
             pltpu.VMEM(observed.shape, F32),
-            pltpu.SMEM(region.shape, jnp.int32),
             pltpu.VMEM(green.shape, F32),
             pltpu.VMEM((freqs, 2, block, 2 * tile), BF16),
             pltpu.VMEM((reach,) + green.shape, F32),
             pltpu.VMEM((slots, freqs, 2, 2 * block, 2 * tile), BF16),
-            pltpu.VMEM((freqs, tiles, slots, own_rows, 2 * block), F32),
-            pltpu.VMEM((freqs, tiles, slots, own_rows, 2 * block), F32),
-            pltpu.VMEM((freqs, tiles, slots, own_rows, 2 * block), F32),
+            pltpu.VMEM((tiles, freqs, own_rows, 2 * block), F32),
+            pltpu.VMEM((tiles, freqs, own_rows, 2 * block), F32),
+            pltpu.VMEM((tiles, freqs, own_rows, 2 * block), F32),
+            pltpu.VMEM((freqs, tiles, reach, own_rows, 2 * block), F32),
+            pltpu.VMEM((freqs, tiles, reach, own_rows, 2 * block), F32),
+            pltpu.VMEM((freqs, tiles, reach, own_rows, 2 * block), F32),
             pltpu.VMEM((2 * block, 2 * block), F32),
             pltpu.VMEM((reach, freqs + 1, own_rows, 2 * block), F32),
             pltpu.VMEM((reach, freqs + 1, own_rows, 2 * block), F32),
             pltpu.VMEM((freqs, tile), F32),
-            pltpu.VMEM((stations, freqs, tile), F32),
             dma,
-            dma((4,)),
+            dma((3,)),
+            dma,
             dma((reach, freqs)), dma((reach, freqs)),
             dma((reach,)), dma((reach,)),
+            dma((tiles,)), dma((tiles,)),
+            dma((tiles,)), dma((tiles,)),
             dma((tiles, freqs)), dma((tiles, freqs)),
             dma((tiles, freqs)), dma((tiles, freqs)),
             dma((stations,)), dma((stations,)),
@@ -322,7 +371,12 @@
         compiler_params=pltpu.CompilerParams(
             collective_id=0, has_side_effects=True, vmem_limit_bytes=60 * 1024 * 1024
         ),
-    )(green, source_power, partners, observed, region)
+    )(green, source_power, partners, observed)
+    mask = jnp.repeat(region.astype(F32), MBLK)
+    summed = totals[0]
+    for k in range(1, stations):
+        summed = summed + totals[k]
+    return summed * (out_scale * mask)[None, :]
 
 
 def solution(mesh):

time: 43.5 us -> 43.7 us (level)
  other arithmetic: 0 us -> 1.36 us
  Pallas kernels: 42 us -> 41.4 us
  local copies, waits for them, and re-layouts: 1.3 us -> 0.73 us
    mul x0 -> x2, other arithmetic: none -> 1.36 us  [shards(): return summed * (out_scale * mask)[None, :]]
    unnamed x1 -> x2, local copies, waits for them, and re-layouts: 1.3 us -> 0.65 us
    pallas_call x1, Pallas kernels: 42 us -> 41.4 us  [shards(): pl.pallas_call(functools.partial(kernel, stations, tiles, reach, c_scale)...]
where the time goes in v3:
time: 43.7 us; the launch traced here: 43.5 us
  Pallas kernels  41.4 us (95%)
  other arithmetic  1.36 us (3%)
  local copies, waits for them, and re-layouts  0.73 us (2%)
    pallas_call x1, Pallas kernels, shards(): pl.pallas_call(functools.partial(kernel, stations, tiles, reach, c_scale)...  41.4 us
    mul x2, other arithmetic, shards(): return summed * (out_scale * mask)[None, :]  1.36 us

profile of v3, /device:TPU:0, one launch (start us, length us, event | category | flops | bytes accessed | tf_op | source)
XLA Modules:
  0.0 43.5 jit_solution(7383681154163569263)
XLA Ops:
  0.0 0.0 copy-start
  0.0 0.7 %copy-done = s32[2]{0:T(128)S(1)} copy-done((s32[2]{0:T(128)S(1)}, s32[2]{0:T(128)}, u32[]{:S(2)}) %copy-start) | copy-done | bytes 32
  0.7 0.1 broadcast_bitcast_fusion
  0.7 41.4 %shard_map.55 = f32[4,8,256]{2,1,0:T(8,128)} custom-call(f32[8,256,128]{2,1,0:T(8,128)} %bitcast.9, f32[8,256]{1,0:T(8,128)} %power_hbm.1, s32[1,2]{1,0:T(1,128)} %partners_hbm.1, f32[1,2,8,64,128]{4,3,2,1,0:T(8,128)} %obs_hbm.1), custom_call_target="tpu_custom_call" | custom-call | tf_op jit(solution)/shard_map/pallas_call | solution.py:337
  42.1 1.4 %bitcast_multiply_fusion = f32[8,256]{1,0:T(8,128)} fusion(f32[4,8,256]{2,1,0:T(8,128)} %shard_map.55, f32[256]{0:T(256)S(1)} %broadcast_bitcast_fusion), kind=kLoop, calls=%fused_computation | loop fusion | flops 8192 | bytes 41984 | tf_op jit(solution)/shard_map/mul | solution.py:379
  (1 shorter events, 0.0 us)
Async XLA Ops:
  0.0 0.7 %copy-start = (s32[2]{0:T(128)S(1)}, s32[2]{0:T(128)}, u32[]{:S(2)}) copy-start(s32[2]{0:T(128)} %param.9) | copy-start | bytes 28

commit v4 on v3

--- a/solution.py
+++ b/solution.py
@@ -373,10 +373,7 @@
         ),
     )(green, source_power, partners, observed)
     mask = jnp.repeat(region.astype(F32), MBLK)
-    summed = totals[0]
-    for k in range(1, stations):
-        summed = summed + totals[k]
-    return summed * (out_scale * mask)[None, :]
+    return jnp.sum(totals, axis=0) * out_scale * mask[None, :]
 
 
 def solution(mesh):

time: 43.7 us -> 43 us (0.984)
  local copies, waits for them, and re-layouts: 0.73 us -> 0.08 us
    reduce_sum x0 -> x1, other arithmetic: none -> 0.77 us  [shards(): return jnp.sum(totals, axis=0) * out_scale * mask[None, :]]
    mul x2, other arithmetic: 1.36 us -> 0.61 us  [shards(): return jnp.sum(totals, axis=0) * out_scale * mask[None, :]]
    unnamed x2, local copies, waits for them, and re-layouts: 0.65 us -> 0.01 us
where the time goes in v4:
time: 43 us; the launch traced here: 42.9 us
  Pallas kernels  41.4 us (96%)
  other arithmetic  1.38 us (3%)
    pallas_call x1, Pallas kernels, shards(): pl.pallas_call(functools.partial(kernel, stations, tiles, reach, c_scale)...  41.4 us

profile of v4, /device:TPU:0, one launch (start us, length us, event | category | flops | bytes accessed | tf_op | source)
XLA Modules:
  0.0 42.9 jit_solution(7288646849455505645)
XLA Ops:
  0.0 41.4 %shard_map.55 = f32[4,8,256]{2,1,0:T(8,128)} custom-call(f32[8,256,128]{2,1,0:T(8,128)} %bitcast.7, f32[8,256]{1,0:T(8,128)} %power_hbm.1, s32[1,2]{1,0:T(1,128)} %partners_hbm.1, f32[1,2,8,64,128]{4,3,2,1,0:T(8,128)} %obs_hbm.1), custom_call_target="tpu_custom_call" | custom-call | tf_op jit(solution)/shard_map/pallas_call | solution.py:337
  41.4 0.0 copy-start
  41.4 0.8 %reduce_sum.9 = f32[8,256]{1,0:T(8,128)S(1)} reduce(f32[4,8,256]{2,1,0:T(8,128)} %shard_map.55, f32[]{:T(128)} %constant.0.clone.1), dimensions={0}, to_apply=%region_0.0 | reduce | flops 6144 | bytes 40964 | tf_op jit(solution)/shard_map/reduce_sum | solution.py:376
  42.2 0.0 copy-done
  42.2 0.1 broadcast_bitcast_fusion
  42.2 0.6 %broadcast_multiply_fusion = f32[8,256]{1,0:T(8,128)} fusion(f32[8,256]{1,0:T(8,128)S(1)} %reduce_sum.9, f32[256]{0:T(256)S(1)} %broadcast_bitcast_fusion), kind=kLoop, calls=%fused_computation | loop fusion | flops 2048 | bytes 17408 | tf_op jit(solution)/shard_map/mul | solution.py:376
  (1 shorter events, 0.0 us)
Async XLA Ops:
  41.4 0.8 %copy-start = (s32[2]{0:T(128)S(1)}, s32[2]{0:T(128)}, u32[]{:S(2)}) copy-start(s32[2]{0:T(128)} %param.9) | copy-start | bytes 28
